TPU v7x, 128 devices: a whole 4x4x4 slice. The times are simulated.
128 devices in a mesh: wide: 32 (over y, x, core), samp: 4 (over z).
Axes of the slice: x: 4, y: 4, z: 4, core: 2. Of those that a mesh axis runs over, the one named last changes fastest.
Arguments:
- features: bfloat16 [4, 128, 96, 128], P('samp', 'wide'), may hold values from -6 to 6
- labels: int32 [4, 128, 96], P('samp', 'wide'), may hold values from 0 to 8
- conv_weight: bfloat16 [3, 3, 128, 128], replicated, may hold values from -0.1875 to 0.1875
- down_weight: bfloat16 [512, 1024], replicated, may hold values from -0.25 to 0.25
- expand_weight: bfloat16 [3, 3, 1024, 2048], P(None, None, None, 'wide'), may hold values from -0.0625 to 0.0625
- reduce_weight: bfloat16 [3, 3, 2048, 1024], P(None, None, 'wide'), may hold values from -0.046875 to 0.046875
- up_weight: bfloat16 [1024, 512], replicated, may hold values from -0.1875 to 0.1875
- class_weight: bfloat16 [128, 9], replicated, may hold values from -3 to 3
Outputs:
- conv_grad: float32 [3, 3, 128, 128], replicated
- down_grad: float32 [512, 1024], replicated
- expand_grad: float32 [3, 3, 1024, 2048], P(None, None, 'samp', 'wide')
- reduce_grad: float32 [3, 3, 2048, 1024], P(None, None, 'wide', 'samp')
- up_grad: float32 [1024, 512], replicated
- class_grad: float32 [128, 9], replicated
All inputs are finite; a program needn't handle non-finite values.
Results may differ from a plain program's by a relative error of at most 0.012.
Values may be sent and summed in bfloat16 or wider, within the bound.
A program may use at most 192 MiB of HBM per device.

v0:
```python
import math
import jax
import jax.numpy as jnp
from jax import lax
from jax.sharding import PartitionSpec as P


def split_up(x, dim, length):
    before, after = (x.shape[:dim], x.shape[dim + 1 :])
    return jnp.moveaxis(x.reshape(*before, length, -1, *after), dim, 0)


def sum_at_owner(x, axis, dim):
    length = lax.axis_size(axis)
    pieces = lax.all_to_all(split_up(x, dim, length), axis, 0, 0, tiled=True)
    return jnp.sum(pieces.astype(jnp.float32), axis=0)


def extended(block, sides, width):
    for axis, dim in sides:
        count = lax.axis_size(axis)
        forward = [(i, i + 1) for i in range(count - 1)]
        backward = [(target, source) for source, target in forward]
        low = lax.ppermute(
            lax.slice_in_dim(block, block.shape[dim] - width, None, axis=dim), axis, forward
        )
        high = lax.ppermute(lax.slice_in_dim(block, 0, width, axis=dim), axis, backward)
        block = jnp.concatenate([low, block, high], axis=dim)
    return block


def silu_slope(value):
    logistic = jax.nn.sigmoid(value)
    return logistic * (1.0 + value * (1.0 - logistic))


def pad_both(values):
    return jnp.pad(values, ((1, 1), (1, 1), (0, 0)))


def to_depth(grid):
    height, across, channels = grid.shape
    blocks = grid.reshape(height // 2, 2, across // 2, 2, channels)
    return jnp.transpose(blocks, (0, 2, 1, 3, 4)).reshape(height // 2, across // 2, 4 * channels)


def from_depth(grid):
    height, across, channels = grid.shape
    blocks = grid.reshape(height, across, 2, 2, channels // 4)
    return jnp.transpose(blocks, (0, 2, 1, 3, 4)).reshape(2 * height, 2 * across, channels // 4)


def taps_in(padded, height, across):
    return jnp.concatenate(
        [padded[p : p + height, q : q + across] for p in range(3) for q in range(3)], axis=-1
    )


def taps_out(values):
    return jnp.concatenate(
        [jnp.pad(values, ((p, 2 - p), (q, 2 - q), (0, 0))) for p in range(3) for q in range(3)],
        axis=-1,
    )


def conv_padded(padded, weight):
    height = padded.shape[0] - 2
    across = padded.shape[1] - 2
    inward = weight.shape[2]
    outward = weight.shape[3]
    if inward <= outward:
        window = taps_in(padded, height, across).reshape(height * across, 9 * inward)
        result = jnp.dot(
            window, weight.reshape(9 * inward, outward), preferred_element_type=jnp.float32
        )
        return result.reshape(height, across, outward)
    flattened = padded.reshape((height + 2) * (across + 2), inward)
    stacked = jnp.transpose(weight, (2, 0, 1, 3)).reshape(inward, 9 * outward)
    spread_out = jnp.dot(flattened, stacked, preferred_element_type=jnp.float32).reshape(
        height + 2, across + 2, 9, outward
    )
    summed = spread_out[0:height, 0:across, 0]
    for offset in range(1, 9):
        p = offset // 3
        q = offset % 3
        summed = summed + spread_out[p : p + height, q : q + across, offset]
    return summed


def correlate(padded, values):
    height, across, outward = values.shape
    inward = padded.shape[-1]
    if inward <= outward:
        window = taps_in(padded, height, across).reshape(height * across, 9 * inward)
        result = lax.dot_general(
            window,
            values.reshape(height * across, outward),
            (((0,), (0,)), ((), ())),
            preferred_element_type=jnp.float32,
        )
        return result.reshape(3, 3, inward, outward)
    shifted = taps_out(values).reshape((height + 2) * (across + 2), 9 * outward)
    result = lax.dot_general(
        padded.reshape(-1, inward),
        shifted,
        (((0,), (0,)), ((), ())),
        preferred_element_type=jnp.float32,
    )
    return jnp.transpose(result.reshape(inward, 3, 3, outward), (1, 2, 0, 3))


def contract_rows(left, right):
    left_flat = left.reshape(-1, left.shape[-1])
    right_flat = right.reshape(-1, right.shape[-1])
    return lax.dot_general(
        left_flat, right_flat, (((0,), (0,)), ((), ())), preferred_element_type=jnp.float32
    )


def flip_kernel(weight):
    return jnp.transpose(weight[::-1, ::-1], (0, 1, 3, 2))


def keep_rows(block_rows, first_row):
    return block_rows


def project_rows(values, weight):
    return jnp.dot(values, weight, preferred_element_type=jnp.float32).astype(jnp.bfloat16)


def widen_rows(values, weight):
    return lax.dot_general(
        values, weight, (((2,), (1,)), ((), ())), preferred_element_type=jnp.float32
    ).astype(jnp.bfloat16)


def collect(values, transform):
    return transform(lax.all_gather(values, "wide", axis=0, tiled=True), jnp.int32(0))


def spread_sum(term_rows, row_total):
    return sum_at_owner(
        term_rows(jnp.int32(0), row_total * lax.axis_size("wide")).astype(jnp.bfloat16), "wide", 0
    )


def local(
    features,
    labels,
    conv_weight,
    down_weight,
    expand_weight,
    reduce_weight,
    up_weight,
    class_weight,
):
    crop_rows = features[0]
    label_map = labels[0]
    height, across, channels = crop_rows.shape
    half_rows = height // 2
    pixel_count = lax.axis_size("wide") * lax.axis_size("samp") * height * across
    loss_scale = 8.0 / math.sqrt(pixel_count)
    classes = lax.broadcasted_iota(jnp.int32, (1, 1, class_weight.shape[1]), 2)
    near_rows = extended(crop_rows, (("wide", 0),), 1)
    padded_in = jnp.pad(near_rows, ((0, 0), (1, 1), (0, 0)))
    hidden_pre = conv_padded(padded_in, conv_weight)
    hidden = jax.nn.silu(hidden_pre).astype(jnp.bfloat16)
    stacked = to_depth(hidden)
    coarse = project_rows(stacked, down_weight)
    coarse_all = collect(coarse, keep_rows)
    coarse_pad = pad_both(coarse_all)
    expand_pre = conv_padded(coarse_pad, expand_weight)
    expanded = jax.nn.silu(expand_pre).astype(jnp.bfloat16)
    expand_pad = pad_both(expanded)

    def reduce_block(first_row, row_count):
        return conv_padded(expand_pad, reduce_weight)

    bottom = (coarse.astype(jnp.float32) + spread_sum(reduce_block, half_rows)).astype(jnp.bfloat16)
    upward = from_depth(jnp.dot(bottom, up_weight, preferred_element_type=jnp.float32))
    joined_pre = upward + hidden.astype(jnp.float32)
    joined = jax.nn.silu(joined_pre).astype(jnp.bfloat16)
    logits = jnp.dot(joined, class_weight, preferred_element_type=jnp.float32)
    exp_logits = jnp.exp(logits)
    probability = exp_logits / jnp.sum(exp_logits, axis=-1, keepdims=True)
    onehot = (label_map[:, :, None] == classes).astype(jnp.float32)
    logit_grad = ((probability - onehot) * loss_scale).astype(jnp.bfloat16)
    class_grad = contract_rows(joined, logit_grad)
    joined_grad = lax.dot_general(
        logit_grad, class_weight, (((2,), (1,)), ((), ())), preferred_element_type=jnp.float32
    )
    upward_grad = (joined_grad * silu_slope(joined_pre)).astype(jnp.bfloat16)
    stacked_grad = to_depth(upward_grad)
    up_grad = contract_rows(bottom, stacked_grad)
    bottom_grad = widen_rows(stacked_grad, up_weight)
    bottom_all = collect(bottom_grad, keep_rows)
    reduce_grad = correlate(expand_pad, bottom_all)
    expanded_back = conv_padded(pad_both(bottom_all), flip_kernel(reduce_weight))
    expanded_grad = (expanded_back * silu_slope(expand_pre)).astype(jnp.bfloat16)
    expand_grad = correlate(coarse_pad, expanded_grad)
    grad_pad = pad_both(expanded_grad)
    back_expand = flip_kernel(expand_weight)

    def expand_back_block(first_row, row_count):
        return conv_padded(grad_pad, back_expand)

    coarse_grad = (
        bottom_grad.astype(jnp.float32) + spread_sum(expand_back_block, half_rows)
    ).astype(jnp.bfloat16)
    down_grad = contract_rows(stacked, coarse_grad)
    down_back = lax.dot_general(
        coarse_grad, down_weight, (((2,), (1,)), ((), ())), preferred_element_type=jnp.float32
    )
    hidden_sum = from_depth(down_back) + upward_grad.astype(jnp.float32)
    hidden_grad = (hidden_sum * silu_slope(hidden_pre)).astype(jnp.bfloat16)
    conv_grad = correlate(padded_in, hidden_grad)
    conv_grad, down_grad, up_grad, class_grad = lax.psum(
        (conv_grad, down_grad, up_grad, class_grad), ("wide", "samp")
    )
    expand_grad, reduce_grad = (
        sum_at_owner(expand_grad.astype(jnp.bfloat16), "samp", 2),
        sum_at_owner(reduce_grad.astype(jnp.bfloat16), "samp", 3),
    )
    return (conv_grad, down_grad, expand_grad, reduce_grad, up_grad, class_grad)


def solution(mesh):
    return jax.shard_map(
        local,
        mesh=mesh,
        in_specs=(
            P("samp", "wide", None, None),
            P("samp", "wide", None),
            P(),
            P(),
            P(None, None, None, "wide"),
            P(None, None, "wide", None),
            P(),
            P(),
        ),
        out_specs=(
            P(),
            P(),
            P(None, None, "samp", "wide"),
            P(None, None, "wide", "samp"),
            P(),
            P(),
        ),
        check_vma=False,
    )
```

profile of v0, /device:TPU:1, one launch (start us, length us, event | category | flops | bytes accessed | tf_op | source)
XLA Modules:
  0.0 589.7 jit_solution(12321008439119090654)
XLA Ops:
  28.2 52.9 %all-gather.3.cloned.1.call-done = bf16[64,48,1024]{2,1,0:T(8,128)(2,1)} async-done(((bf16[2,48,1024]{2,1,0:T(8,128)(2,1)}), bf16[64,48,1024]{2,1,0:T(8,128)(2,1)}) %all-gather.3.cloned.1.call-update) | async-done | bytes 6291472 | tf_op jit(solution)/shard_map/all_gather | solution.py:139
  81.1 6.3 %copy.56 = bf16[64,48,1024]{2,0,1:T(8,128)(2,1)S(1)} copy(bf16[64,48,1024]{2,1,0:T(8,128)(2,1)} %all-gather.3.cloned.1.call-done) | data formatting | bytes 12582912 | tf_op jit(solution)/shard_map/all_gather | solution.py:139
  87.4 11.4 %fusion.1 = f32[66,50,9,64]{0,3,2,1:T(8,128)} fusion(bf16[9,64,1024,1]{2,1,0,3:T(8,128)(2,1)S(1)} %bitcast.176, bf16[64,48,1024]{2,0,1:T(8,128)(2,1)S(1)} %copy.56), kind=kOutput, calls=%fused_computation.3 | convolution fusion | flops 3892838400 | bytes 15074304 | tf_op jit(solution)/shard_map/dot_general | solution.py:79
  98.8 7.6 %multiply_convert_fusion = (bf16[64,48,64]{0,2,1:T(8,128)(2,1)S(1)}, f32[64,48,64]{0,2,1:T(8,128)S(1)}) fusion(f32[66,50,9,64]{0,3,2,1:T(8,128)} %fusion.1), kind=kLoop, calls=%fused_computation.34 | loop fusion | flops 2555904 | bytes 8257536 | tf_op jit(solution)/shard_map/convert_element_type | solution.py:174
  117.2 10.7 %copy.57 = bf16[64,48,576]{2,1,0:T(8,128)(2,1)} copy(bf16[64,48,576]{0,2,1:T(8,128)(2,1)} %slice_dynamic-update-slice_fusion.8) | data formatting | bytes 7077888 | tf_op jit(solution)/shard_map/concatenate | solution.py:54
  127.9 7.1 %convolution_convert_fusion.1 = bf16[64,48,1024]{2,1,0:T(8,128)(2,1)S(1)} fusion(bf16[64,48,576]{2,1,0:T(8,128)(2,1)} %copy.57, bf16[576,1024,1]{1,0,2:T(8,128)(2,1)} %bitcast.177), kind=kOutput, calls=%fused_computation.11 | convolution fusion | flops 3627024384 | bytes 11010048 | tf_op jit(solution)/shard_map/dot_general | solution.py:73
  135.0 78.0 %all_to_all.20 = bf16[32,2,48,1024]{3,2,1,0:T(8,128)(2,1)S(1)} all-to-all(bf16[32,2,48,1024]{3,2,1,0:T(8,128)(2,1)S(1)} %bitcast.166), channel_id=1, replica_groups=mesh['wide'=32,'samp'=4] {'wide'}, dimensions={0} | all-to-all | bytes 12582912 | tf_op jit(solution)/shard_map/all_to_all | solution.py:15
  222.2 43.3 %all-gather.5.cloned.1.call-done = bf16[64,48,1024]{2,1,0:T(8,128)(2,1)} async-done(((bf16[2,48,1024]{2,1,0:T(8,128)(2,1)}), bf16[64,48,1024]{2,1,0:T(8,128)(2,1)}) %all-gather.5.cloned.1.call-update) | async-done | bytes 6291472 | tf_op jit(solution)/shard_map/all_gather | solution.py:139
  265.4 6.4 %copy.60 = bf16[64,48,1024]{2,0,1:T(8,128)(2,1)S(1)} copy(bf16[64,48,1024]{2,1,0:T(8,128)(2,1)} %all-gather.5.cloned.1.call-done) | data formatting | bytes 12582912 | tf_op jit(solution)/shard_map/all_gather | solution.py:139
  271.9 8.4 %fusion.3 = f32[66,50,9,64]{0,3,1,2:T(8,128)S(1)} fusion(bf16[9,64,1024,1]{2,1,3,0:T(8,128)(2,1)S(1)} %bitcast.179, bf16[64,48,1024]{2,0,1:T(8,128)(2,1)S(1)} %copy.60), kind=kOutput, calls=%fused_computation.5 | convolution fusion | flops 3892838400 | bytes 15074304 | tf_op jit(solution)/shard_map/dot_general | solution.py:79
  293.6 10.7 %copy.70 = bf16[64,48,576]{2,1,0:T(8,128)(2,1)} copy(bf16[64,48,576]{0,2,1:T(8,128)(2,1)} %slice_dynamic-update-slice_fusion) | data formatting | bytes 7077888 | tf_op jit(solution)/shard_map/concatenate | solution.py:54
  304.3 9.1 %convolution_convert_fusion = bf16[64,48,1024]{2,1,0:T(8,128)(2,1)} fusion(bf16[64,48,576]{2,1,0:T(8,128)(2,1)} %copy.70, bf16[576,1024,1]{1,0,2:T(8,128)(2,1)S(1)} %bitcast.178), kind=kOutput, calls=%fused_computation.10 | convolution fusion | flops 3627024384 | bytes 11010048 | tf_op jit(solution)/shard_map/dot_general | solution.py:73
  313.4 5.4 all-to-all-start.1
  320.8 6.3 %copy.91 = bf16[64,48,1024]{2,1,0:T(8,128)(2,1)S(1)} copy(bf16[64,48,1024]{2,0,1:T(8,128)(2,1)} %copy-done.2) | data formatting | bytes 12582912
  327.1 7.7 %pad.52.clone = bf16[66,50,1024]{2,1,0:T(8,128)(2,1)} pad(bf16[64,48,1024]{2,1,0:T(8,128)(2,1)S(1)} %copy.91, bf16[]{:T(256)} %constant.4.clone.1), padding=1_1x1_1x0_0 | pad | bytes 13049858 | tf_op jit(solution)/shard_map/jit(_pad)/pad | solution.py:38
  334.8 9.4 %reshape.180 = bf16[3300,1024,1,1]{1,0,2,3:T(8,128)(2,1)} reshape(bf16[66,50,1024]{2,1,0:T(8,128)(2,1)} %pad.52.clone) | data formatting | bytes 13516800 | tf_op jit(solution)/shard_map/reshape | solution.py:77
  344.2 6.2 %copy.77 = bf16[576,3072]{1,0:T(8,128)(2,1)} copy(bf16[576,3072]{0,1:T(8,128)(2,1)} %bitcast.163) | data formatting | bytes 7077888 | tf_op jit(solution)/shard_map/dot_general | solution.py:95
  352.2 7.7 %convolution_convert_fusion.2 = bf16[3,3,64,1024]{3,2,1,0:T(8,128)(2,1)S(1)} fusion(bf16[3,3,64,3072]{3,2,1,0:T(8,128)(2,1)} %bitcast.168, bf16[3072,1024,1,1]{1,0,3,2:T(8,128)(2,1)} %bitcast.164), kind=kOutput, calls=%fused_computation.37 | convolution fusion | flops 3624468480 | bytes 11010048 | tf_op jit(solution)/shard_map/dot_general | solution.py:95
  372.1 12.9 %copy.73 = bf16[66,50,576]{2,1,0:T(8,128)(2,1)} copy(bf16[66,50,576]{0,2,1:T(8,128)(2,1)} %pad_dynamic-update-slice_fusion) | data formatting | bytes 7603200 | tf_op jit(solution)/shard_map/concatenate | solution.py:60
  385.0 7.9 %reshape.155 = bf16[3300,576]{1,0:T(8,128)(2,1)} reshape(bf16[66,50,576]{2,1,0:T(8,128)(2,1)} %copy.73) | data formatting | bytes 7603200 | tf_op jit(solution)/shard_map/reshape | solution.py:102
  392.9 6.4 %copy.74 = bf16[576,3300]{1,0:T(8,128)(2,1)} copy(bf16[576,3300]{0,1:T(8,128)(2,1)} %bitcast.162) | data formatting | bytes 7603200 | tf_op jit(solution)/shard_map/dot_general | solution.py:103
  413.9 8.2 %fusion.12 = bf16[1024,3,3,64]{0,3,2,1:T(8,128)(2,1)S(1)} fusion(bf16[3,3,64,3300]{3,2,1,0:T(8,128)(2,1)} %bitcast.167, bf16[3300,1024,1,1]{1,0,2,3:T(8,128)(2,1)} %reshape.180), kind=kOutput, calls=%fused_computation.36 | convolution fusion | flops 3893428224 | bytes 11739648 | tf_op jit(solution)/shard_map/dot_general | solution.py:103
  427.7 77.0 %psum.31 = f32[128,9]{0,1:T(8,128)} all-reduce(f32[128,9]{0,1:T(8,128)S(1)} %convolution_bitcast_fusion), channel_id=1, replica_groups=mesh['wide'=32,'samp'=4] {'wide','samp'}, use_global_device_ids=true, to_apply=%region_8.9 | all-reduce | flops 1152 | bytes 9216 | tf_op jit(solution)/shard_map/psum | solution.py:218
  506.7 69.6 %all-reduce.16.cloned.1.call-done = (f32[3,3,128,128]{3,2,1,0:T(8,128)}, f32[512,1024]{1,0:T(8,128)}, f32[1024,512]{1,0:T(8,128)}) async-done(((f32[3,3,128,128]{3,2,1,0:T(8,128)}, f32[512,1024]{1,0:T(8,128)}, f32[1024,512]{1,0:T(8,128)}), (f32[3,3,128,128]{3,2,1,0:T(8,128)}, f32[512,1024]{1,0:T(8,128)}, f32[1024,512]{1,0:T(8,128)})) %all-reduce.16.cloned.1.call-update) | async-done | bytes 4784144 | tf_op jit(solution)/shard_map/psum | solution.py:218
  (146 shorter events, 98.6 us)
Async XLA Ops:
  7.2 207.5 %copy-start = (bf16[1024,512]{1,0:T(8,128)(2,1)S(1)}, bf16[1024,512]{1,0:T(8,128)(2,1)}, u32[]{:S(2)}) copy-start(bf16[1024,512]{1,0:T(8,128)(2,1)} %param.14) | copy-start | bytes 3145732
  7.2 73.9 %all-gather.3.cloned.1.call-start = ((), (), s32[]{:S(2)}) async-start(), calls=%async_computation.4 | async-start | bytes 6488064 | tf_op jit(solution)/shard_map/all_gather | solution.py:139
  8.1 6.4 %collective-permute-start = (bf16[1,96,128]{2,1,0:T(8,128)(2,1)S(1)}, bf16[1,96,128]{2,1,0:T(8,128)(2,1)S(1)}, u32[]{:S(2)}, u32[]{:S(2)}) collective-permute-start(bf16[1,96,128]{2,1,0:T(8,128)(2,1)S(1)} %get-tuple-element.22), channel_id=1, source_target_pairs={{0,4},{4,8},{8,12},{12,16},{16,20},{20,24},{24,28},{28,32},{32,36}... | collective-permute-start | bytes 73736 | tf_op jit(solution)/shard_map/ppermute | solution.py:24
  12.6 5.1 collective-permute-start.1
  28.1 59.3 %copy-start.8 = (bf16[3,3,1024,64]{2,3,1,0:T(8,128)(2,1)S(1)}, bf16[3,3,1024,64]{2,3,1,0:T(8,128)(2,1)}, u32[]{:S(2)}) copy-start(bf16[3,3,1024,64]{2,3,1,0:T(8,128)(2,1)} %param.12) | copy-start | bytes 3538948
  28.1 237.3 %all-gather.5.cloned.1.call-start = ((), (), s32[]{:S(2)}) async-start(), calls=%async_computation.5 | async-start | bytes 6488064 | tf_op jit(solution)/shard_map/all_gather | solution.py:139
  87.4 11.4 %copy-start.2 = (bf16[64,48,1024]{2,0,1:T(8,128)(2,1)}, bf16[64,48,1024]{2,0,1:T(8,128)(2,1)S(1)}, u32[]{:S(2)}) copy-start(bf16[64,48,1024]{2,0,1:T(8,128)(2,1)S(1)} %copy.56) | copy-start | bytes 18874372
  216.2 55.7 %copy-start.11 = (bf16[4,96,128]{2,1,0:T(8,128)(2,1)}, bf16[4,96,128]{2,1,0:T(8,128)(2,1)S(1)}, u32[]{:S(2)}) copy-start(bf16[4,96,128]{2,1,0:T(8,128)(2,1)S(1)} %fusion.15) | copy-start | bytes 294916
  265.4 6.4 %copy-start.10 = (bf16[3,3,64,1024]{3,2,1,0:T(8,128)(2,1)S(1)}, bf16[3,3,64,1024]{3,2,1,0:T(8,128)(2,1)}, u32[]{:S(2)}) copy-start(bf16[3,3,64,1024]{3,2,1,0:T(8,128)(2,1)} %rev.6) | copy-start | bytes 3538948
  292.4 11.9 %copy-start.9 = (bf16[3,3,1024,64]{2,3,1,0:T(8,128)(2,1)S(1)}, bf16[3,3,1024,64]{2,3,1,0:T(8,128)(2,1)}, u32[]{:S(2)}) copy-start(bf16[3,3,1024,64]{2,3,1,0:T(8,128)(2,1)} %rev.7) | copy-start | bytes 3538948
  313.4 6.2 %copy-start.15 = (bf16[4,96,128]{2,1,0:T(8,128)(2,1)S(1)}, bf16[4,96,128]{2,1,0:T(8,128)(2,1)}, u32[]{:S(2)}) copy-start(bf16[4,96,128]{2,1,0:T(8,128)(2,1)} %get-tuple-element.19) | copy-start | bytes 294916
  313.4 6.3 %copy-start.14 = (bf16[4,96,128]{2,1,0:T(8,128)(2,1)S(1)}, bf16[4,96,128]{2,1,0:T(8,128)(2,1)}, u32[]{:S(2)}) copy-start(bf16[4,96,128]{2,1,0:T(8,128)(2,1)} %get-tuple-element.18) | copy-start | bytes 294916
  313.4 6.3 %copy-start.4 = (bf16[1,4,96,128]{3,2,1,0:T(8,128)(2,1)S(1)}, bf16[1,4,96,128]{3,2,1,0:T(8,128)(2,1)}, u32[]{:S(2)}) copy-start(bf16[1,4,96,128]{3,2,1,0:T(8,128)(2,1)} %param.8) | copy-start | bytes 294916
  313.4 6.3 %copy-start.13 = (bf16[4,96,128]{2,1,0:T(8,128)(2,1)S(1)}, bf16[4,96,128]{2,1,0:T(8,128)(2,1)}, u32[]{:S(2)}) copy-start(bf16[4,96,128]{2,1,0:T(8,128)(2,1)} %get-tuple-element.17) | copy-start | bytes 294916
  313.4 6.4 %copy-start.12 = (bf16[4,96,128]{2,1,0:T(8,128)(2,1)S(1)}, bf16[4,96,128]{2,1,0:T(8,128)(2,1)}, u32[]{:S(2)}) copy-start(bf16[4,96,128]{2,1,0:T(8,128)(2,1)} %get-tuple-element.16) | copy-start | bytes 294916
  313.4 6.4 %copy-start.17 = (bf16[4,96,128]{2,1,0:T(8,128)(2,1)S(1)}, bf16[4,96,128]{2,1,0:T(8,128)(2,1)}, u32[]{:S(2)}) copy-start(bf16[4,96,128]{2,1,0:T(8,128)(2,1)} %get-tuple-element.12) | copy-start | bytes 294916
  313.4 85.8 %all-to-all-start.1 = ((bf16[32,2,48,1024]{3,2,1,0:T(8,128)(2,1)}), bf16[32,2,48,1024]{3,2,1,0:T(8,128)(2,1)}, u32[]{:S(2)}, u32[]{:S(2)}) async-start(bf16[32,2,48,1024]{3,2,1,0:T(8,128)(2,1)} %bitcast.165), calls=%async_computation.1 | async-start | bytes 12582912 | tf_op jit(solution)/shard_map/all_to_all | solution.py:15
  399.2 8.9 %copy-start.6 = (bf16[2,48,1024]{2,1,0:T(8,128)(2,1)S(1)}, bf16[2,48,1024]{2,1,0:T(8,128)(2,1)}, u32[]{:S(2)}) copy-start(bf16[2,48,1024]{2,1,0:T(8,128)(2,1)} %convolution_convert_fusion.3) | copy-start | bytes 589828
  399.2 9.0 %copy-start.3 = (bf16[512,1024]{1,0:T(8,128)(2,1)S(1)}, bf16[512,1024]{1,0:T(8,128)(2,1)}, u32[]{:S(2)}) copy-start(bf16[512,1024]{1,0:T(8,128)(2,1)} %param.11) | copy-start | bytes 3145732
  399.3 24.0 %all-to-all-start.3 = ((bf16[4,3,3,64,256]{4,3,2,1,0:T(8,128)(2,1)}), bf16[4,3,3,64,256]{4,3,2,1,0:T(8,128)(2,1)S(1)}, u32[]{:S(2)}, u32[]{:S(2)}) async-start(bf16[4,3,3,64,256]{4,3,2,1,0:T(8,128)(2,1)} %bitcast.157), calls=%async_computation.3 | async-start | bytes 2359296 | tf_op jit(solution)/shard_map/all_to_all | solution.py:15
  403.5 172.8 %all-reduce.16.cloned.1.call-start = ((), (), s32[]{:S(2)}) async-start(), calls=%async_computation.6 | async-start | bytes 9568256 | tf_op jit(solution)/shard_map/psum | solution.py:218
  413.9 13.6 %copy-start.20 = (bf16[4,96,128]{2,1,0:T(8,128)(2,1)S(1)}, bf16[4,96,128]{2,1,0:T(8,128)(2,1)}, u32[]{:S(2)}) copy-start(bf16[4,96,128]{2,1,0:T(8,128)(2,1)} %copy-done.19) | copy-start | bytes 294916
  423.2 82.5 %all-to-all-start.2 = ((bf16[4,3,3,256,64]{3,4,2,1,0:T(8,128)(2,1)}), bf16[4,3,3,256,64]{3,4,2,1,0:T(8,128)(2,1)S(1)}, u32[]{:S(2)}, u32[]{:S(2)}) async-start(bf16[4,3,3,256,64]{3,4,2,1,0:T(8,128)(2,1)} %bitcast.159), calls=%async_computation.2 | async-start | bytes 2359296 | tf_op jit(solution)/shard_map/all_to_all | solution.py:15
  427.7 155.2 %copy-start.1 = (bf16[1024,512]{1,0:T(8,128)(2,1)S(1)}, bf16[1024,512]{1,0:T(8,128)(2,1)}, u32[]{:S(2)}) copy-start(bf16[1024,512]{1,0:T(8,128)(2,1)} %param.14) | copy-start | bytes 3145732
  (7 other events, 24.8 us)
Sparse Core Ops, SparseCore 0:
  28.2 52.8 all-gather.2
  217.6 47.8 all-gather.4
  414.0 162.2 all-reduce.15
where the time goes:
time: 596 us; the launch traced here: 590 us
  waiting for transfers between devices  169 us (28%)
  blocking collectives  155 us (26%)
  local copies, waits for them, and re-layouts  143 us (24%)
  matrix products  64.2 us (11%)
  other arithmetic  23.4 us (4%)
  starting transfers between devices  20.7 us (3%)
  between operations  14.6 us (2%)
    all_gather x2, waiting for transfers between devices, collect(): lax.all_gather(values, 'wide', axis=0, tiled=True)  96.2 us
    all_to_all x1, blocking collectives, sum_at_owner(): pieces = lax.all_to_all(split_up(x, dim, length), axis, 0, 0, tiled=True)  78 us
    psum x1, blocking collectives, local(): lax.psum((conv_grad, down_grad, up_grad, class_grad), ('wide', 'samp'))  77 us
    psum x1, waiting for transfers between devices, local(): lax.psum((conv_grad, down_grad, up_grad, class_grad), ('wide', 'samp'))  69.6 us
    unnamed x88, local copies, waits for them, and re-layouts  43.5 us
    concatenate x6, local copies, waits for them, and re-layouts, taps_in(): jnp.concatenate([padded[p:p + height, q:q + across] for p in range(3) for...  24.7 us
    dot_general x2, matrix products, conv_padded(): jnp.dot(flattened, stacked, preferred_element_type=jnp.float32)  19.8 us
    dot_general x3, matrix products, conv_padded(): jnp.dot(window, weight.reshape(9 * inward, outward), preferred_element_ty...  18.2 us
  transfers between devices with their start and end apart: 8, of which 4 were waited for; matrix products, arithmetic and copies ran while one was open for 18% of the time, Pallas kernels for 0%

commit v1 on v0

--- a/solution.py
+++ b/solution.py
@@ -3,6 +3,12 @@
 import jax.numpy as jnp
 from jax import lax
 from jax.sharding import PartitionSpec as P
+
+
+def recover_the_heads(frame_in, ax_name):
+    t_next = jnp.stack(lax.psum(1, ax_name) * [frame_in], 0)
+    formed = jnp.concatenate(lax.all_to_all(t_next, ax_name, 0, 0), 0)
+    return formed
 
 
 def split_up(x, dim, length):
@@ -136,7 +142,7 @@
 
 
 def collect(values, transform):
-    return transform(lax.all_gather(values, "wide", axis=0, tiled=True), jnp.int32(0))
+    return transform(recover_the_heads(values, "wide"), jnp.int32(0))
 
 
 def spread_sum(term_rows, row_total):

time: 596 us -> 690 us (1.16)
  blocking collectives: 155 us -> 237 us
  local copies, waits for them, and re-layouts: 143 us -> 181 us
  waiting for transfers between devices: 169 us -> 141 us
  starting transfers between devices: 20.7 us -> 31.2 us
    all_gather x2 -> x0, waiting for transfers between devices: 96.2 us -> none  [collect(): lax.all_gather(values, 'wide', axis=0, tiled=True)]
    all_to_all x0 -> x1, blocking collectives: none -> 82.1 us  [recover_the_heads(): formed = jnp.concatenate(lax.all_to_all(t_next, ax_name, 0, 0), 0)]
    all_to_all x0 -> x1, waiting for transfers between devices: none -> 68.3 us  [recover_the_heads(): formed = jnp.concatenate(lax.all_to_all(t_next, ax_name, 0, 0), 0)]
    reshape x0 -> x2, local copies, waits for them, and re-layouts: none -> 20.5 us  [recover_the_heads(): formed = jnp.concatenate(lax.all_to_all(t_next, ax_name, 0, 0), 0)]
    all_to_all x0 -> x3, local copies, waits for them, and re-layouts: none -> 17.2 us  [recover_the_heads(): formed = jnp.concatenate(lax.all_to_all(t_next, ax_name, 0, 0), 0)]
    all_gather x2 -> x0, local copies, waits for them, and re-layouts: 12.7 us -> none  [collect(): lax.all_gather(values, 'wide', axis=0, tiled=True)]
    another operation x0 -> x2, local copies, waits for them, and re-layouts: none -> 12.4 us  [recover_the_heads(): t_next = jnp.stack(lax.psum(1, ax_name) * [frame_in], 0)]
  transfers between devices with their start and end apart: 8 -> 7, of which waited for: 4 -> 3; matrix products, arithmetic and copies ran while one was open for 18% -> 16% of each run, Pallas kernels for 0% -> 0%
where the time goes in v1:
time: 690 us; the launch traced here: 684 us
  blocking collectives  237 us (34%)
  local copies, waits for them, and re-layouts  181 us (26%)
  waiting for transfers between devices  141 us (20%)
  matrix products  60.3 us (9%)
  starting transfers between devices  31.2 us (5%)
  other arithmetic  18.3 us (3%)
  between operations  14.9 us (2%)
    all_to_all x1, blocking collectives, recover_the_heads(): formed = jnp.concatenate(lax.all_to_all(t_next, ax_name, 0, 0), 0)  82.1 us
    all_to_all x1, blocking collectives, sum_at_owner(): pieces = lax.all_to_all(split_up(x, dim, length), axis, 0, 0, tiled=True)  78.1 us
    psum x1, blocking collectives, local(): lax.psum((conv_grad, down_grad, up_grad, class_grad), ('wide', 'samp'))  77.2 us
    psum x1, waiting for transfers between devices, local(): lax.psum((conv_grad, down_grad, up_grad, class_grad), ('wide', 'samp'))  69.4 us
    all_to_all x1, waiting for transfers between devices, recover_the_heads(): formed = jnp.concatenate(lax.all_to_all(t_next, ax_name, 0, 0), 0)  68.3 us
    unnamed x88, local copies, waits for them, and re-layouts  44.1 us
    concatenate x6, local copies, waits for them, and re-layouts, taps_in(): jnp.concatenate([padded[p:p + height, q:q + across] for p in range(3) for...  24.8 us
    dot_general x2, matrix products, conv_padded(): jnp.dot(flattened, stacked, preferred_element_type=jnp.float32)  21 us
  transfers between devices with their start and end apart: 7, of which 3 were waited for; matrix products, arithmetic and copies ran while one was open for 16% of the time, Pallas kernels for 0%

profile of v1, /device:TPU:1, one launch (start us, length us, event | category | flops | bytes accessed | tf_op | source)
XLA Modules:
  0.0 684.2 jit_solution(15252693164859389674)
XLA Ops:
  33.4 82.1 %all_to_all.30 = bf16[32,2,48,1024]{3,1,2,0:T(2,128)(2,1)S(1)} all-to-all(bf16[32,2,48,1024]{3,1,2,0:T(2,128)(2,1)S(1)} %stack.4), channel_id=1, replica_groups=mesh['wide'=32,'samp'=4] {'wide'}, dimensions={0} | all-to-all | bytes 12582912 | tf_op jit(solution)/shard_map/all_to_all | solution.py:10
  120.9 10.3 %reshape.147 = bf16[64,48,1024]{2,0,1:T(8,128)(2,1)} reshape(bf16[32,2,48,1024]{3,1,0,2:T(2,128)(2,1)} %copy.60) | data formatting | bytes 12582912 | tf_op jit(solution)/shard_map/reshape | solution.py:10
  131.1 10.3 %fusion.1 = f32[66,50,9,64]{0,3,2,1:T(8,128)S(1)} fusion(bf16[9,64,1024,1]{2,1,0,3:T(8,128)(2,1)S(1)} %bitcast.180, bf16[64,48,1024]{2,0,1:T(8,128)(2,1)} %reshape.147), kind=kOutput, calls=%fused_computation.3 | convolution fusion | flops 3892838400 | bytes 15074304 | tf_op jit(solution)/shard_map/dot_general | solution.py:85
  154.8 10.7 %copy.61 = bf16[64,48,576]{2,1,0:T(8,128)(2,1)} copy(bf16[64,48,576]{0,2,1:T(8,128)(2,1)} %slice_dynamic-update-slice_fusion.8) | data formatting | bytes 7077888 | tf_op jit(solution)/shard_map/concatenate | solution.py:60
  165.5 7.1 %convolution_convert_fusion.1 = bf16[64,48,1024]{2,1,0:T(8,128)(2,1)S(1)} fusion(bf16[64,48,576]{2,1,0:T(8,128)(2,1)} %copy.61, bf16[576,1024,1]{1,0,2:T(8,128)(2,1)} %bitcast.181), kind=kOutput, calls=%fused_computation.11 | convolution fusion | flops 3627024384 | bytes 11010048 | tf_op jit(solution)/shard_map/dot_general | solution.py:79
  172.6 78.1 %all_to_all.31 = bf16[32,2,48,1024]{3,2,1,0:T(8,128)(2,1)S(1)} all-to-all(bf16[32,2,48,1024]{3,2,1,0:T(8,128)(2,1)S(1)} %bitcast.170), channel_id=1, replica_groups=mesh['wide'=32,'samp'=4] {'wide'}, dimensions={0} | all-to-all | bytes 12582912 | tf_op jit(solution)/shard_map/all_to_all | solution.py:21
  255.1 6.6 stack.5
  271.4 68.3 %all-to-all-done.2 = bf16[32,2,48,1024]{3,1,2,0:T(2,128)(2,1)} async-done(((bf16[32,2,48,1024]{3,1,2,0:T(2,128)(2,1)}), bf16[32,2,48,1024]{3,1,2,0:T(2,128)(2,1)}, u32[]{:S(2)}, u32[]{:S(2)}) %all-to-all-start.2) | async-done | bytes 6291488 | tf_op jit(solution)/shard_map/all_to_all | solution.py:10
  339.7 6.8 copy.65
  346.4 10.2 %reshape.155 = bf16[64,48,1024]{2,0,1:T(8,128)(2,1)} reshape(bf16[32,2,48,1024]{3,1,0,2:T(2,128)(2,1)} %copy.65) | data formatting | bytes 12582912 | tf_op jit(solution)/shard_map/reshape | solution.py:10
  356.7 10.7 %fusion.3 = f32[66,50,9,64]{0,3,1,2:T(8,128)S(1)} fusion(bf16[9,64,1024,1]{2,1,3,0:T(8,128)(2,1)} %bitcast.183, bf16[64,48,1024]{2,0,1:T(8,128)(2,1)} %reshape.155), kind=kOutput, calls=%fused_computation.5 | convolution fusion | flops 3892838400 | bytes 15074304 | tf_op jit(solution)/shard_map/dot_general | solution.py:85
  380.7 10.7 %copy.75 = bf16[64,48,576]{2,1,0:T(8,128)(2,1)} copy(bf16[64,48,576]{0,2,1:T(8,128)(2,1)} %slice_dynamic-update-slice_fusion) | data formatting | bytes 7077888 | tf_op jit(solution)/shard_map/concatenate | solution.py:60
  391.4 9.0 %convolution_convert_fusion = bf16[64,48,1024]{2,1,0:T(8,128)(2,1)} fusion(bf16[64,48,576]{2,1,0:T(8,128)(2,1)} %copy.75, bf16[576,1024,1]{1,0,2:T(8,128)(2,1)S(1)} %bitcast.182), kind=kOutput, calls=%fused_computation.10 | convolution fusion | flops 3627024384 | bytes 11010048 | tf_op jit(solution)/shard_map/dot_general | solution.py:79
  400.5 10.3 %all-to-all-start.3 = ((bf16[32,2,48,1024]{3,2,1,0:T(8,128)(2,1)}), bf16[32,2,48,1024]{3,2,1,0:T(8,128)(2,1)}, u32[]{:S(2)}, u32[]{:S(2)}) async-start(bf16[32,2,48,1024]{3,2,1,0:T(8,128)(2,1)} %bitcast.168), calls=%async_computation.3 | async-start | bytes 12582912 | tf_op jit(solution)/shard_map/all_to_all | solution.py:21
  412.7 6.3 copy.97
  419.0 7.7 %pad.52.clone = bf16[66,50,1024]{2,1,0:T(8,128)(2,1)} pad(bf16[64,48,1024]{2,1,0:T(8,128)(2,1)S(1)} %copy.97, bf16[]{:T(256)} %constant.4.clone.1), padding=1_1x1_1x0_0 | pad | bytes 13049858 | tf_op jit(solution)/shard_map/jit(_pad)/pad | solution.py:44
  426.7 9.4 %reshape.188 = bf16[3300,1024,1,1]{1,0,2,3:T(8,128)(2,1)} reshape(bf16[66,50,1024]{2,1,0:T(8,128)(2,1)} %pad.52.clone) | data formatting | bytes 13516800 | tf_op jit(solution)/shard_map/reshape | solution.py:83
  436.1 6.3 copy.82
  465.5 12.9 %copy.78 = bf16[66,50,576]{2,1,0:T(8,128)(2,1)} copy(bf16[66,50,576]{0,2,1:T(8,128)(2,1)} %pad_dynamic-update-slice_fusion) | data formatting | bytes 7603200 | tf_op jit(solution)/shard_map/concatenate | solution.py:66
  478.4 7.9 %reshape.164 = bf16[3300,576]{1,0:T(8,128)(2,1)} reshape(bf16[66,50,576]{2,1,0:T(8,128)(2,1)} %copy.78) | data formatting | bytes 7603200 | tf_op jit(solution)/shard_map/reshape | solution.py:108
  486.3 6.3 copy.79
  508.1 8.2 %fusion.12 = bf16[1024,3,3,64]{0,3,2,1:T(8,128)(2,1)S(1)} fusion(bf16[3,3,64,3300]{3,2,1,0:T(8,128)(2,1)} %bitcast.171, bf16[3300,1024,1,1]{1,0,2,3:T(8,128)(2,1)} %reshape.188), kind=kOutput, calls=%fused_computation.36 | convolution fusion | flops 3893428224 | bytes 11739648 | tf_op jit(solution)/shard_map/dot_general | solution.py:109
  521.9 77.2 %psum.31 = f32[128,9]{0,1:T(8,128)} all-reduce(f32[128,9]{0,1:T(8,128)S(1)} %convolution_bitcast_fusion), channel_id=1, replica_groups=mesh['wide'=32,'samp'=4] {'wide','samp'}, use_global_device_ids=true, to_apply=%region_8.9 | all-reduce | flops 1152 | bytes 9216 | tf_op jit(solution)/shard_map/psum | solution.py:224
  601.1 69.4 %all-reduce.16.cloned.1.call-done = (f32[3,3,128,128]{3,2,1,0:T(8,128)}, f32[512,1024]{1,0:T(8,128)}, f32[1024,512]{1,0:T(8,128)}) async-done(((f32[3,3,128,128]{3,2,1,0:T(8,128)}, f32[512,1024]{1,0:T(8,128)}, f32[1024,512]{1,0:T(8,128)}), (f32[3,3,128,128]{3,2,1,0:T(8,128)}, f32[512,1024]{1,0:T(8,128)}, f32[1024,512]{1,0:T(8,128)})) %all-reduce.16.cloned.1.call-update) | async-done | bytes 4784144 | tf_op jit(solution)/shard_map/psum | solution.py:224
  (150 shorter events, 126.6 us)
Async XLA Ops:
  7.2 245.2 %copy-start = (bf16[1024,512]{1,0:T(8,128)(2,1)S(1)}, bf16[1024,512]{1,0:T(8,128)(2,1)}, u32[]{:S(2)}) copy-start(bf16[1024,512]{1,0:T(8,128)(2,1)} %param.14) | copy-start | bytes 3145732
  8.0 6.4 collective-permute-start
  12.5 5.1 collective-permute-start.1
  120.9 10.3 %copy-start.6 = (bf16[3,3,1024,64]{2,3,1,0:T(8,128)(2,1)S(1)}, bf16[3,3,1024,64]{2,3,1,0:T(8,128)(2,1)}, u32[]{:S(2)}) copy-start(bf16[3,3,1024,64]{2,3,1,0:T(8,128)(2,1)} %param.12) | copy-start | bytes 3538948
  253.9 7.8 %copy-start.8 = (bf16[2,2,48,2,128]{4,3,1,2,0:T(2,128)(2,1)}, bf16[2,2,48,2,128]{4,3,1,2,0:T(2,128)(2,1)S(1)}, u32[]{:S(2)}) copy-start(bf16[2,2,48,2,128]{4,3,1,2,0:T(2,128)(2,1)S(1)} %copy.100) | copy-start | bytes 294916
  261.7 77.9 %all-to-all-start.2 = ((bf16[32,2,48,1024]{3,1,2,0:T(2,128)(2,1)}), bf16[32,2,48,1024]{3,1,2,0:T(2,128)(2,1)}, u32[]{:S(2)}, u32[]{:S(2)}) async-start(bf16[32,2,48,1024]{3,1,2,0:T(2,128)(2,1)} %stack.5), calls=%async_computation.2 | async-start | bytes 12582912 | tf_op jit(solution)/shard_map/all_to_all | solution.py:10
  379.4 11.9 %copy-start.7 = (bf16[3,3,1024,64]{2,3,1,0:T(8,128)(2,1)S(1)}, bf16[3,3,1024,64]{2,3,1,0:T(8,128)(2,1)}, u32[]{:S(2)}) copy-start(bf16[3,3,1024,64]{2,3,1,0:T(8,128)(2,1)} %rev.7) | copy-start | bytes 3538948
  400.4 11.0 %copy-start.16 = (bf16[4,96,128]{2,1,0:T(8,128)(2,1)S(1)}, bf16[4,96,128]{2,1,0:T(8,128)(2,1)}, u32[]{:S(2)}) copy-start(bf16[4,96,128]{2,1,0:T(8,128)(2,1)} %get-tuple-element.20) | copy-start | bytes 294916
  400.4 11.1 %copy-start.18 = (bf16[4,96,128]{2,1,0:T(8,128)(2,1)S(1)}, bf16[4,96,128]{2,1,0:T(8,128)(2,1)}, u32[]{:S(2)}) copy-start(bf16[4,96,128]{2,1,0:T(8,128)(2,1)} %get-tuple-element.14) | copy-start | bytes 294916
  400.4 11.1 %copy-start.15 = (bf16[4,96,128]{2,1,0:T(8,128)(2,1)S(1)}, bf16[4,96,128]{2,1,0:T(8,128)(2,1)}, u32[]{:S(2)}) copy-start(bf16[4,96,128]{2,1,0:T(8,128)(2,1)} %get-tuple-element.19) | copy-start | bytes 294916
  400.4 11.1 %copy-start.14 = (bf16[4,96,128]{2,1,0:T(8,128)(2,1)S(1)}, bf16[4,96,128]{2,1,0:T(8,128)(2,1)}, u32[]{:S(2)}) copy-start(bf16[4,96,128]{2,1,0:T(8,128)(2,1)} %get-tuple-element.18) | copy-start | bytes 294916
  400.4 11.2 %copy-start.4 = (bf16[1,4,96,128]{3,2,1,0:T(8,128)(2,1)S(1)}, bf16[1,4,96,128]{3,2,1,0:T(8,128)(2,1)}, u32[]{:S(2)}) copy-start(bf16[1,4,96,128]{3,2,1,0:T(8,128)(2,1)} %param.8) | copy-start | bytes 294916
  400.5 11.2 %copy-start.13 = (bf16[4,96,128]{2,1,0:T(8,128)(2,1)S(1)}, bf16[4,96,128]{2,1,0:T(8,128)(2,1)}, u32[]{:S(2)}) copy-start(bf16[4,96,128]{2,1,0:T(8,128)(2,1)} %get-tuple-element.17) | copy-start | bytes 294916
  400.5 11.2 %copy-start.12 = (bf16[4,96,128]{2,1,0:T(8,128)(2,1)S(1)}, bf16[4,96,128]{2,1,0:T(8,128)(2,1)}, u32[]{:S(2)}) copy-start(bf16[4,96,128]{2,1,0:T(8,128)(2,1)} %get-tuple-element.16) | copy-start | bytes 294916
  400.5 11.3 %copy-start.17 = (bf16[4,96,128]{2,1,0:T(8,128)(2,1)S(1)}, bf16[4,96,128]{2,1,0:T(8,128)(2,1)}, u32[]{:S(2)}) copy-start(bf16[4,96,128]{2,1,0:T(8,128)(2,1)} %get-tuple-element.12) | copy-start | bytes 294916
  400.5 11.3 %copy-start.11 = (bf16[4,96,128]{2,1,0:T(8,128)(2,1)S(1)}, bf16[4,96,128]{2,1,0:T(8,128)(2,1)}, u32[]{:S(2)}) copy-start(bf16[4,96,128]{2,1,0:T(8,128)(2,1)} %get-tuple-element.21) | copy-start | bytes 294916
  400.5 92.1 %all-to-all-start.3 = ((bf16[32,2,48,1024]{3,2,1,0:T(8,128)(2,1)}), bf16[32,2,48,1024]{3,2,1,0:T(8,128)(2,1)}, u32[]{:S(2)}, u32[]{:S(2)}) async-start(bf16[32,2,48,1024]{3,2,1,0:T(8,128)(2,1)} %bitcast.168), calls=%async_computation.3 | async-start | bytes 12582912 | tf_op jit(solution)/shard_map/all_to_all | solution.py:21
  436.1 6.3 copy-start.9
  492.6 9.8 %copy-start.2 = (bf16[512,1024]{1,0:T(8,128)(2,1)S(1)}, bf16[512,1024]{1,0:T(8,128)(2,1)}, u32[]{:S(2)}) copy-start(bf16[512,1024]{1,0:T(8,128)(2,1)} %param.11) | copy-start | bytes 3145732
  492.6 24.9 %all-to-all-start.5 = ((bf16[4,3,3,64,256]{4,3,2,1,0:T(8,128)(2,1)}), bf16[4,3,3,64,256]{4,3,2,1,0:T(8,128)(2,1)S(1)}, u32[]{:S(2)}, u32[]{:S(2)}) async-start(bf16[4,3,3,64,256]{4,3,2,1,0:T(8,128)(2,1)} %bitcast.161), calls=%async_computation.5 | async-start | bytes 2359296 | tf_op jit(solution)/shard_map/all_to_all | solution.py:21
  497.7 172.8 %all-reduce.16.cloned.1.call-start = ((), (), s32[]{:S(2)}) async-start(), calls=%async_computation.6 | async-start | bytes 9568256 | tf_op jit(solution)/shard_map/psum | solution.py:224
  508.1 13.6 %copy-start.20 = (bf16[4,96,128]{2,1,0:T(8,128)(2,1)S(1)}, bf16[4,96,128]{2,1,0:T(8,128)(2,1)}, u32[]{:S(2)}) copy-start(bf16[4,96,128]{2,1,0:T(8,128)(2,1)} %copy-done.19) | copy-start | bytes 294916
  517.5 82.6 %all-to-all-start.4 = ((bf16[4,3,3,256,64]{3,4,2,1,0:T(8,128)(2,1)}), bf16[4,3,3,256,64]{3,4,2,1,0:T(8,128)(2,1)S(1)}, u32[]{:S(2)}, u32[]{:S(2)}) async-start(bf16[4,3,3,256,64]{3,4,2,1,0:T(8,128)(2,1)} %bitcast.163), calls=%async_computation.4 | async-start | bytes 2359296 | tf_op jit(solution)/shard_map/all_to_all | solution.py:21
  521.9 155.1 %copy-start.1 = (bf16[1024,512]{1,0:T(8,128)(2,1)S(1)}, bf16[1024,512]{1,0:T(8,128)(2,1)}, u32[]{:S(2)}) copy-start(bf16[1024,512]{1,0:T(8,128)(2,1)} %param.14) | copy-start | bytes 3145732
  (6 other events, 16.6 us)
Sparse Core Ops, SparseCore 0:
  508.2 162.2 all-reduce.15
